TPU v7x, 512 devices: a whole 4x8x8 slice. The times are simulated.
512 devices in a mesh: row: 8 (over y), col: 16 (over x_lo, z), layer: 4 (over x_hi, core).
Axes of the slice: x: 4 (x_hi: 2, x_lo: 2; x = x_hi * 2 + x_lo), y: 8, z: 8, core: 2. Of those that a mesh axis runs over, the one named last changes fastest.
Arguments:
- integrals: bfloat16 [64, 1024, 3072], P('layer', 'col', 'row'), may hold values from -0.0234375 to 0.0234375
- amplitudes: bfloat16 [64, 1024, 2048], P('layer', 'row', 'col'), may hold values from -6 to 6
- coulomb: bfloat16 [3072, 2048], P(('row', 'layer'), 'col'), may hold values from -6 to 6
- row_gap: float32 [3072], P(('row', 'layer')), may hold values from 0.5 to 4
- col_gap: float32 [2048], P('col'), may hold values from 0.5 to 4
Outputs:
- residual: float32 [3072, 2048], P(('row', 'layer'), 'col')
All inputs are finite; a program needn't handle non-finite values.
Results may differ from a plain program's by a relative error of at most 0.0003.
Values may be sent and summed in bfloat16 or wider, within the bound.
No kernel may reach another device: no remote copies, remote signals or barrier semaphores. Data moves between devices by JAX's collectives and lax.ppermute only.
A program may use at most 64 MiB of HBM per device.

v0:
```python
import jax
import jax.numpy as jnp
from jax import lax
from jax.sharding import PartitionSpec as P


def local(integrals, amplitudes, coulomb, row_gap, col_gap):
    contract = (((0, 1), (0, 1)), ((), ()))
    gathered = lax.all_gather(amplitudes, "row", axis=1, tiled=True)
    partial_sum = lax.dot_general(
        lax.all_gather(integrals, "col", axis=1, tiled=True),
        gathered,
        contract,
        preferred_element_type=jnp.float32,
    )
    share_rows = coulomb.shape[0]
    summed_all = lax.psum(partial_sum, "layer")
    own_rows = lax.dynamic_slice_in_dim(
        summed_all, lax.axis_index("layer") * share_rows, share_rows, 0
    )
    gap_sum = row_gap[:, None] + col_gap[None, :]
    return (coulomb.astype(jnp.float32) + own_rows) / gap_sum


def solution(mesh):
    placed = (
        P("layer", "col", "row"),
        P("layer", "row", "col"),
        P(("row", "layer"), "col"),
        P(("row", "layer")),
        P("col"),
    )
    return jax.shard_map(
        local, mesh=mesh, in_specs=placed, out_specs=P(("row", "layer"), "col"), check_vma=False
    )
```

profile of v0, /device:TPU:1, one launch (start us, length us, event | category | flops | bytes accessed | tf_op | source)
XLA Modules:
  0.0 286.8 jit_solution(3546155924513565021)
XLA Ops:
  6.5 0.0 copy-start
  6.5 0.0 copy-start.1
  6.5 0.0 copy-start.2
  6.5 0.0 all-gather.5.cloned.1.call-start
  6.5 0.7 all-gather.5.cloned.1.call-update
  7.3 0.0 all-gather.3.cloned.1.call-start
  7.3 0.7 all-gather.3.cloned.1.call-update
  8.0 0.0 all-reduce.2.cloned.1.call-start
  8.1 64.0 %all-gather.5.cloned.1.call-done = bf16[16,1024,128]{2,1,0:T(8,128)(2,1)} async-done(((bf16[16,128,128]{2,1,0:T(8,128)(2,1)}), bf16[16,1024,128]{2,1,0:T(8,128)(2,1)}) %all-gather.5.cloned.1.call-update) | async-done | bytes 4194320 | tf_op jit(solution)/shard_map/all_gather | solution.py:9
  72.1 147.7 %all-gather.3.cloned.1.call-done = bf16[16,1024,384]{2,1,0:T(8,128)(2,1)} async-done(((bf16[16,64,384]{2,1,0:T(8,128)(2,1)}), bf16[16,1024,384]{2,1,0:T(8,128)(2,1)}) %all-gather.3.cloned.1.call-update) | async-done | bytes 12582928 | tf_op jit(solution)/shard_map/all_gather | solution.py:11
  219.8 9.9 %convolution_bitcast_fusion = f32[384,128]{1,0:T(8,128)} fusion(bf16[16,1024,384]{2,1,0:T(8,128)(2,1)} %all-gather.3.cloned.1.call-done, bf16[16,1024,128]{2,1,0:T(8,128)(2,1)} %all-gather.5.cloned.1.call-done), kind=kOutput, calls=%fused_computation | convolution fusion | flops 1610612736 | bytes 16973824 | tf_op jit(solution)/shard_map/dot_general | solution.py:10
  229.7 0.0 all-reduce.2.cloned.1.call-update
  229.7 49.0 %all-reduce.2.cloned.1.call-done = f32[384,128]{1,0:T(8,128)} async-done(((f32[384,128]{1,0:T(8,128)}), f32[384,128]{1,0:T(8,128)}) %all-reduce.2.cloned.1.call-update) | async-done | bytes 196624 | tf_op jit(solution)/shard_map/psum | solution.py:17
  278.7 0.0 copy-done
  278.7 0.0 copy-done.1
  278.7 0.0 copy-done.2
  278.7 1.5 add_divide_fusion
Async XLA Ops:
  6.5 272.2 %copy-start = (bf16[96,128]{1,0:T(8,128)(2,1)S(1)}, bf16[96,128]{1,0:T(8,128)(2,1)}, u32[]{:S(2)}) copy-start(bf16[96,128]{1,0:T(8,128)(2,1)} %param.7) | copy-start | bytes 73732
  6.5 272.2 %copy-start.1 = (f32[128]{0:T(128)S(1)}, f32[128]{0:T(128)}, u32[]{:S(2)}) copy-start(f32[128]{0:T(128)} %param.9) | copy-start | bytes 1540
  6.5 272.2 %copy-start.2 = (f32[96]{0:T(128)S(1)}, f32[96]{0:T(128)}, u32[]{:S(2)}) copy-start(f32[96]{0:T(128)} %param.8) | copy-start | bytes 1156
  6.5 65.6 %all-gather.5.cloned.1.call-start = ((), (), s32[]{:S(2)}) async-start(), calls=%async_computation.1 | async-start | bytes 4718592 | tf_op jit(solution)/shard_map/all_gather | solution.py:9
  7.3 212.5 %all-gather.3.cloned.1.call-start = ((), (), s32[]{:S(2)}) async-start(), calls=%async_computation | async-start | bytes 13369344 | tf_op jit(solution)/shard_map/all_gather | solution.py:11
  8.0 270.7 %all-reduce.2.cloned.1.call-start = ((), (), s32[]{:S(2)}) async-start(), calls=%async_computation.2 | async-start | bytes 393216 | tf_op jit(solution)/shard_map/psum | solution.py:17
Sparse Core Ops, SparseCore 0:
  9.4 62.6 all-gather.4
  74.2 145.5 all-gather.2
  229.8 48.8 all-reduce.1
where the time goes:
time: 287 us
  waiting for transfers between devices  262 us (91%)
  between operations  13.1 us (5%)
  matrix products  9.89 us (3%)
    all_gather x1, waiting for transfers between devices, local(): lax.all_gather(integrals, 'col', axis=1, tiled=True)  148 us
    all_gather x1, waiting for transfers between devices, local(): gathered = lax.all_gather(amplitudes, 'row', axis=1, tiled=True)  64 us
    psum x1, waiting for transfers between devices, local(): summed_all = lax.psum(partial_sum, 'layer')  49 us
    dot_general x1, matrix products, local(): lax.dot_general(lax.all_gather(integrals, 'col', axis=1, tiled=True), gat...  9.89 us
  transfers between devices with their start and end apart: 3, of which 3 were waited for; matrix products, arithmetic and copies ran while one was open for 0% of the time, Pallas kernels for 0%

commit v1 on v0

--- a/solution.py
+++ b/solution.py
@@ -6,7 +6,12 @@
 
 def local(integrals, amplitudes, coulomb, row_gap, col_gap):
     contract = (((0, 1), (0, 1)), ((), ()))
-    gathered = lax.all_gather(amplitudes, "row", axis=1, tiled=True)
+    ring = [amplitudes]
+    for hop in range(7):
+        ring.append(lax.ppermute(ring[-1], "row", [(dev, (dev + 1) % 8) for dev in range(8)]))
+    gathered = jnp.roll(
+        jnp.concatenate(ring[::-1], axis=1), (lax.axis_index("row") + 1) * ring[0].shape[1], axis=1
+    )
     partial_sum = lax.dot_general(
         lax.all_gather(integrals, "col", axis=1, tiled=True),
         gathered,

time: 287 us -> 231 us (0.80)
  waiting for transfers between devices: 262 us -> 165 us
  local copies, waits for them, and re-layouts: 0.01 us -> 20 us
  starting transfers between devices: 0.08 us -> 19.1 us
    all_gather x1, waiting for transfers between devices: 148 us -> 40.1 us  [local(): lax.all_gather(integrals, 'col', axis=1, tiled=True)]
    ppermute x0 -> x7, waiting for transfers between devices: none -> 75 us  [local(): lax.ppermute(ring[-1], 'row', [(dev, (dev + 1) % 8) for dev in range(8)])]
    all_gather x1 -> x0, waiting for transfers between devices: 64 us -> none  [local(): gathered = lax.all_gather(amplitudes, 'row', axis=1, tiled=True)]
    unnamed x6 -> x22, local copies, waits for them, and re-layouts: 0.01 us -> 19.1 us
    ppermute x0 -> x7, starting transfers between devices: none -> 19 us  [local(): lax.ppermute(ring[-1], 'row', [(dev, (dev + 1) % 8) for dev in range(8)])]
  transfers between devices with their start and end apart: 3 -> 9, of which waited for: 3 -> 9; matrix products, arithmetic and copies ran while one was open for 0% -> 9% of each run, Pallas kernels for 0% -> 0%
where the time goes in v1:
time: 231 us; the launch traced here: 230 us
  waiting for transfers between devices  165 us (71%)
  local copies, waits for them, and re-layouts  20 us (9%)
  starting transfers between devices  19.1 us (8%)
  between operations  13.5 us (6%)
  matrix products  11.5 us (5%)
    ppermute x7, waiting for transfers between devices, local(): lax.ppermute(ring[-1], 'row', [(dev, (dev + 1) % 8) for dev in range(8)])  75 us
    psum x1, waiting for transfers between devices, local(): summed_all = lax.psum(partial_sum, 'layer')  49 us
    all_gather x1, waiting for transfers between devices, local(): lax.all_gather(integrals, 'col', axis=1, tiled=True)  40.1 us
    unnamed x22, local copies, waits for them, and re-layouts  19.1 us
    ppermute x7, starting transfers between devices, local(): lax.ppermute(ring[-1], 'row', [(dev, (dev + 1) % 8) for dev in range(8)])  19 us
    dot_general x1, matrix products, local(): lax.dot_general(lax.all_gather(integrals, 'col', axis=1, tiled=True), gat...  11.5 us
  transfers between devices with their start and end apart: 9, of which 9 were waited for; matrix products, arithmetic and copies ran while one was open for 9% of the time, Pallas kernels for 0%

profile of v1, /device:TPU:1, one launch (start us, length us, event | category | flops | bytes accessed | tf_op | source)
XLA Modules:
  0.0 230.4 jit_solution(1171871287431351955)
XLA Ops:
  7.3 1.3 copy.11
  8.6 4.0 %collective-permute-start = (bf16[16,128,128]{1,2,0:T(8,128)(2,1)S(1)}, bf16[16,128,128]{1,2,0:T(8,128)(2,1)S(1)}, u32[]{:S(2)}, u32[]{:S(2)}) collective-permute-start(bf16[16,128,128]{1,2,0:T(8,128)(2,1)S(1)} %copy.11), channel_id=1, source_target_pairs={{0,64},{64,128},{128,192},{192,256},{256,320},{320,384},{384,448},... | collective-permute-start | bytes 1572872 | tf_op jit(solution)/shard_map/ppermute | solution.py:11
  12.7 8.4 %collective-permute-done = bf16[16,128,128]{1,2,0:T(8,128)(2,1)S(1)} collective-permute-done((bf16[16,128,128]{1,2,0:T(8,128)(2,1)S(1)}, bf16[16,128,128]{1,2,0:T(8,128)(2,1)S(1)}, u32[]{:S(2)}, u32[]{:S(2)}) %collective-permute-start) | collective-permute-done | bytes 524320 | tf_op jit(solution)/shard_map/ppermute | solution.py:11
  21.1 5.3 %collective-permute-start.1 = (bf16[16,128,128]{1,2,0:T(8,128)(2,1)S(1)}, bf16[16,128,128]{1,2,0:T(8,128)(2,1)S(1)}, u32[]{:S(2)}, u32[]{:S(2)}) collective-permute-start(bf16[16,128,128]{1,2,0:T(8,128)(2,1)S(1)} %collective-permute-done), channel_id=1, source_target_pairs={{0,64},{64,128},{128,192},{192,256},{256,320},{320,384},{384,448},... | collective-permute-start | bytes 1572872 | tf_op jit(solution)/shard_map/ppermute | solution.py:11
  26.4 11.7 %collective-permute-done.1 = bf16[16,128,128]{1,2,0:T(8,128)(2,1)S(1)} collective-permute-done((bf16[16,128,128]{1,2,0:T(8,128)(2,1)S(1)}, bf16[16,128,128]{1,2,0:T(8,128)(2,1)S(1)}, u32[]{:S(2)}, u32[]{:S(2)}) %collective-permute-start.1) | collective-permute-done | bytes 524320 | tf_op jit(solution)/shard_map/ppermute | solution.py:11
  38.2 2.0 collective-permute-start.2
  40.2 11.4 %collective-permute-done.2 = bf16[16,128,128]{1,2,0:T(8,128)(2,1)S(1)} collective-permute-done((bf16[16,128,128]{1,2,0:T(8,128)(2,1)S(1)}, bf16[16,128,128]{1,2,0:T(8,128)(2,1)S(1)}, u32[]{:S(2)}, u32[]{:S(2)}) %collective-permute-start.2) | collective-permute-done | bytes 524320 | tf_op jit(solution)/shard_map/ppermute | solution.py:11
  51.6 1.9 collective-permute-start.3
  53.5 10.3 %collective-permute-done.3 = bf16[16,128,128]{1,2,0:T(8,128)(2,1)S(1)} collective-permute-done((bf16[16,128,128]{1,2,0:T(8,128)(2,1)S(1)}, bf16[16,128,128]{1,2,0:T(8,128)(2,1)S(1)}, u32[]{:S(2)}, u32[]{:S(2)}) %collective-permute-start.3) | collective-permute-done | bytes 524320 | tf_op jit(solution)/shard_map/ppermute | solution.py:11
  63.8 1.9 collective-permute-start.4
  65.7 13.0 %collective-permute-done.4 = bf16[16,128,128]{1,2,0:T(8,128)(2,1)S(1)} collective-permute-done((bf16[16,128,128]{1,2,0:T(8,128)(2,1)S(1)}, bf16[16,128,128]{1,2,0:T(8,128)(2,1)S(1)}, u32[]{:S(2)}, u32[]{:S(2)}) %collective-permute-start.4) | collective-permute-done | bytes 524320 | tf_op jit(solution)/shard_map/ppermute | solution.py:11
  78.7 1.9 collective-permute-start.5
  80.6 10.4 %collective-permute-done.5 = bf16[16,128,128]{1,2,0:T(8,128)(2,1)} collective-permute-done((bf16[16,128,128]{1,2,0:T(8,128)(2,1)S(1)}, bf16[16,128,128]{1,2,0:T(8,128)(2,1)}, u32[]{:S(2)}, u32[]{:S(2)}) %collective-permute-start.5) | collective-permute-done | bytes 524320 | tf_op jit(solution)/shard_map/ppermute | solution.py:11
  91.0 1.9 collective-permute-start.6
  92.9 9.8 %collective-permute-done.6 = bf16[16,128,128]{1,2,0:T(8,128)(2,1)} collective-permute-done((bf16[16,128,128]{1,2,0:T(8,128)(2,1)}, bf16[16,128,128]{1,2,0:T(8,128)(2,1)}, u32[]{:S(2)}, u32[]{:S(2)}) %collective-permute-start.6) | collective-permute-done | bytes 524320 | tf_op jit(solution)/shard_map/ppermute | solution.py:11
  102.7 2.0 constant_dynamic-update-slice_fusion.15
  104.7 2.0 constant_dynamic-update-slice_fusion.14
  112.1 2.0 constant_dynamic-update-slice_fusion.7
  114.0 2.0 constant_dynamic-update-slice_fusion.6
  120.5 0.9 constant_dynamic-update-slice_fusion
  121.4 40.1 %all-gather.2.cloned.1.call-done = bf16[16,1024,384]{2,1,0:T(8,128)(2,1)} async-done(((bf16[16,64,384]{2,1,0:T(8,128)(2,1)}), bf16[16,1024,384]{2,1,0:T(8,128)(2,1)}) %all-gather.2.cloned.1.call-update) | async-done | bytes 12582928 | tf_op jit(solution)/shard_map/all_gather | solution.py:16
  161.5 11.5 %fusion.2 = f32[384,128]{1,0:T(8,128)} fusion(bf16[16,1024,384]{2,1,0:T(8,128)(2,1)} %all-gather.2.cloned.1.call-done, bf16[16,2048,128]{1,2,0:T(8,128)(2,1)} %constant_dynamic-update-slice_fusion, s32[]{:T(128)S(6)} %select_n.17), kind=kOutput, calls=%fused_computation.2 | convolution fusion | flops 1610612736 | bytes 16973828 | tf_op jit(solution)/shard_map/dot_general | solution.py:15
  173.0 49.0 %all-reduce.2.cloned.1.call-done = f32[384,128]{1,0:T(8,128)} async-done(((f32[384,128]{1,0:T(8,128)}), f32[384,128]{1,0:T(8,128)}) %all-reduce.2.cloned.1.call-update) | async-done | bytes 196624 | tf_op jit(solution)/shard_map/psum | solution.py:22
  222.1 1.5 add_divide_fusion
  (21 shorter events, 10.6 us)
Async XLA Ops:
  6.5 155.0 %all-gather.2.cloned.1.call-start = ((), (), s32[]{:S(2)}) async-start(), calls=%async_computation | async-start | bytes 13369344 | tf_op jit(solution)/shard_map/all_gather | solution.py:16
  7.3 214.8 %all-reduce.2.cloned.1.call-start = ((), (), s32[]{:S(2)}) async-start(), calls=%async_computation.1 | async-start | bytes 393216 | tf_op jit(solution)/shard_map/psum | solution.py:22
  8.6 12.5 %collective-permute-start = (bf16[16,128,128]{1,2,0:T(8,128)(2,1)S(1)}, bf16[16,128,128]{1,2,0:T(8,128)(2,1)S(1)}, u32[]{:S(2)}, u32[]{:S(2)}) collective-permute-start(bf16[16,128,128]{1,2,0:T(8,128)(2,1)S(1)} %copy.11), channel_id=1, source_target_pairs={{0,64},{64,128},{128,192},{192,256},{256,320},{320,384},{384,448},... | collective-permute-start | bytes 1572872 | tf_op jit(solution)/shard_map/ppermute | solution.py:11
  21.1 17.0 %collective-permute-start.1 = (bf16[16,128,128]{1,2,0:T(8,128)(2,1)S(1)}, bf16[16,128,128]{1,2,0:T(8,128)(2,1)S(1)}, u32[]{:S(2)}, u32[]{:S(2)}) collective-permute-start(bf16[16,128,128]{1,2,0:T(8,128)(2,1)S(1)} %collective-permute-done), channel_id=1, source_target_pairs={{0,64},{64,128},{128,192},{192,256},{256,320},{320,384},{384,448},... | collective-permute-start | bytes 1572872 | tf_op jit(solution)/shard_map/ppermute | solution.py:11
  38.2 13.4 %collective-permute-start.2 = (bf16[16,128,128]{1,2,0:T(8,128)(2,1)S(1)}, bf16[16,128,128]{1,2,0:T(8,128)(2,1)S(1)}, u32[]{:S(2)}, u32[]{:S(2)}) collective-permute-start(bf16[16,128,128]{1,2,0:T(8,128)(2,1)S(1)} %collective-permute-done.1), channel_id=1, source_target_pairs={{0,64},{64,128},{128,192},{192,256},{256,320},{320,384},{384,448},... | collective-permute-start | bytes 1572872 | tf_op jit(solution)/shard_map/ppermute | solution.py:11
  51.6 12.2 %collective-permute-start.3 = (bf16[16,128,128]{1,2,0:T(8,128)(2,1)S(1)}, bf16[16,128,128]{1,2,0:T(8,128)(2,1)S(1)}, u32[]{:S(2)}, u32[]{:S(2)}) collective-permute-start(bf16[16,128,128]{1,2,0:T(8,128)(2,1)S(1)} %collective-permute-done.2), channel_id=1, source_target_pairs={{0,64},{64,128},{128,192},{192,256},{256,320},{320,384},{384,448},... | collective-permute-start | bytes 1572872 | tf_op jit(solution)/shard_map/ppermute | solution.py:11
  63.8 14.9 %collective-permute-start.4 = (bf16[16,128,128]{1,2,0:T(8,128)(2,1)S(1)}, bf16[16,128,128]{1,2,0:T(8,128)(2,1)S(1)}, u32[]{:S(2)}, u32[]{:S(2)}) collective-permute-start(bf16[16,128,128]{1,2,0:T(8,128)(2,1)S(1)} %collective-permute-done.3), channel_id=1, source_target_pairs={{0,64},{64,128},{128,192},{192,256},{256,320},{320,384},{384,448},... | collective-permute-start | bytes 1572872 | tf_op jit(solution)/shard_map/ppermute | solution.py:11
  78.7 12.3 %collective-permute-start.5 = (bf16[16,128,128]{1,2,0:T(8,128)(2,1)S(1)}, bf16[16,128,128]{1,2,0:T(8,128)(2,1)}, u32[]{:S(2)}, u32[]{:S(2)}) collective-permute-start(bf16[16,128,128]{1,2,0:T(8,128)(2,1)S(1)} %collective-permute-done.4), channel_id=1, source_target_pairs={{0,64},{64,128},{128,192},{192,256},{256,320},{320,384},{384,448},... | collective-permute-start | bytes 1572872 | tf_op jit(solution)/shard_map/ppermute | solution.py:11
  91.0 11.7 %collective-permute-start.6 = (bf16[16,128,128]{1,2,0:T(8,128)(2,1)}, bf16[16,128,128]{1,2,0:T(8,128)(2,1)}, u32[]{:S(2)}, u32[]{:S(2)}) collective-permute-start(bf16[16,128,128]{1,2,0:T(8,128)(2,1)} %collective-permute-done.5), channel_id=1, source_target_pairs={{0,64},{64,128},{128,192},{192,256},{256,320},{320,384},{384,448},... | collective-permute-start | bytes 1572872 | tf_op jit(solution)/shard_map/ppermute | solution.py:11
  121.4 100.7 %copy-start = (bf16[96,128]{1,0:T(8,128)(2,1)S(1)}, bf16[96,128]{1,0:T(8,128)(2,1)}, u32[]{:S(2)}) copy-start(bf16[96,128]{1,0:T(8,128)(2,1)} %param.7) | copy-start | bytes 73732
  121.4 100.7 %copy-start.1 = (f32[128]{0:T(128)S(1)}, f32[128]{0:T(128)}, u32[]{:S(2)}) copy-start(f32[128]{0:T(128)} %param.9) | copy-start | bytes 1540
  121.4 100.7 %copy-start.2 = (f32[96]{0:T(128)S(1)}, f32[96]{0:T(128)}, u32[]{:S(2)}) copy-start(f32[96]{0:T(128)} %param.8) | copy-start | bytes 1156
Sparse Core Ops, SparseCore 0:
  9.4 151.9 all-gather.1
  173.1 48.8 all-reduce.1
